TPU v7x, 128 devices: a whole 4x4x4 slice. The times are simulated.
128 devices in a mesh: ctx: 32 (over y, x_lo, z), pb: 4 (over x_hi, core).
Axes of the slice: x: 4 (x_hi: 2, x_lo: 2; x = x_hi * 2 + x_lo), y: 4, z: 4, core: 2. Of those that a mesh axis runs over, the one named last changes fastest.
Arguments:
- queries: bfloat16 [512, 128, 576], P('pb'), may hold values from -69 to 69
- key_cache: bfloat16 [16384, 576], P('ctx'), may hold values from -12 to 12
- index_queries: bfloat16 [64, 512, 128], P(None, 'pb'), may hold values from -47 to 47
- index_keys: bfloat16 [16384, 128], P('ctx'), may hold values from -12 to 12
- head_weights: float32 [512, 64], P('pb'), may hold values from 0.02 to 0.3
- positions: int32 [512], P('pb'), may hold values from 4096 to 16383
- valid_lengths: int32 [512], P('pb'), may hold values from 3 to 16384
Outputs:
- kl_loss: float32 [512], P('pb')
- key_grad: float32 [16384, 128], P('ctx')
- query_grad: float32 [64, 512, 128], P('ctx', 'pb')
- weight_grad: float32 [512, 64], P('pb')
All inputs are finite; a program needn't handle non-finite values.
Results may differ from a plain program's by a relative error of at most 0.0023.
Values sent between devices are 32-bit elements; how exact they have to be, the bound alone decides.
A program may use at most 192 MiB of HBM per device.

v0:
```python
import jax
import jax.numpy as jnp
from jax import lax
from jax.sharding import PartitionSpec as P

NEG = -1e30
main_scale = 192 ** (-0.5)


def local(queries, key_cache, index_queries, index_keys, head_weights, positions, valid_lengths):
    q_rows, head_count, lat_width = queries.shape
    s_rows = key_cache.shape[0]
    group_count = head_count // 16
    first_key = lax.axis_index("ctx") * s_rows
    key_index = first_key + jnp.arange(s_rows, dtype=jnp.int32)
    valid_mask = (key_index[None, :] <= positions[:, None]) & (
        key_index[None, :] > (positions - valid_lengths)[:, None]
    )
    iscale = index_keys.shape[1] ** (-0.5)
    loss_scale = s_rows * lax.axis_size("ctx") / (q_rows * lax.axis_size("pb"))

    def group_scores(group_id):
        query_block = lax.dynamic_slice_in_dim(queries, group_id * 16, 16, 1)
        scores = (
            jnp.einsum("qhc,tc->qht", query_block, key_cache, preferred_element_type=jnp.float32)
            * main_scale
        )
        return jnp.where(valid_mask[:, None, :], scores, NEG)

    def group_expo(group_id):
        scores = group_scores(group_id)
        row_peak = jnp.max(scores, axis=2)
        expo = jnp.where(valid_mask[:, None, :], jnp.exp(scores - row_peak[:, :, None]), 0.0)
        return (row_peak, expo)

    def stats_kept(group_id):
        row_peak, expo = group_expo(group_id)
        return (row_peak, jnp.sum(expo, axis=2), expo)

    peaks, sums, kept = lax.map(stats_kept, jnp.arange(group_count))
    main_peak = peaks.transpose(1, 0, 2).reshape(q_rows, head_count)
    main_total = sums.transpose(1, 0, 2).reshape(q_rows, head_count)
    own_peak = main_peak
    index_raw = jnp.einsum(
        "jqd,td->jqt", index_queries, index_keys, preferred_element_type=jnp.float32
    )
    active = jnp.maximum(index_raw, 0.0)
    logits = jnp.sum(head_weights.T[:, :, None] * active, axis=0) * iscale
    logits = jnp.where(valid_mask, logits, NEG)
    index_peak = jnp.max(logits, axis=1)
    index_total = jnp.sum(jnp.where(valid_mask, jnp.exp(logits - index_peak[:, None]), 0.0), axis=1)
    global_main, global_index = lax.pmax((main_peak, index_peak), "ctx")
    main_total, index_total = lax.psum(
        (
            main_total * jnp.exp(main_peak - global_main),
            index_total * jnp.exp(index_peak - global_index),
        ),
        "ctx",
    )
    main_peak, index_peak = (global_main, global_index)
    factor = (
        (jnp.exp(own_peak - main_peak) / main_total)
        .reshape(q_rows, group_count, 16)
        .transpose(1, 0, 2)
    )

    def add_kept(group_id, running):
        return running + jnp.sum(kept[group_id] * factor[group_id][:, :, None], axis=1)

    target = (
        lax.fori_loop(0, group_count, add_kept, jnp.zeros((q_rows, s_rows), jnp.float32))
        / head_count
    )
    log_index = logits - index_peak[:, None] - jnp.log(index_total)[:, None]
    index_prob = jnp.where(
        valid_mask, jnp.exp(logits - index_peak[:, None]) / index_total[:, None], 0.0
    )
    positive = valid_mask & (target > 0)
    safe_target = jnp.where(target > 0, target, 1.0)
    loss_local = jnp.sum(
        jnp.where(positive, target * (jnp.log(safe_target) - log_index), 0.0), axis=1
    )
    dlogit = jnp.where(valid_mask, loss_scale * (index_prob - target), 0.0)
    weight_local = jnp.sum(dlogit[None] * active, axis=2).T * iscale
    coefficient = jnp.where(
        index_raw > 0, dlogit[None] * head_weights.T[:, :, None] * iscale, 0.0
    ).astype(jnp.bfloat16)
    kl_loss, weight_grad = lax.psum((loss_local, weight_local), "ctx")
    key_local = jnp.einsum(
        "jqt,jqd->td", coefficient, index_queries, preferred_element_type=jnp.float32
    )
    query_grad = lax.psum_scatter(
        jnp.einsum("jqt,td->jqd", coefficient, index_keys, preferred_element_type=jnp.float32),
        "ctx",
        scatter_dimension=0,
        tiled=True,
    )
    key_grad = lax.psum(key_local, "pb")
    return (kl_loss, key_grad, query_grad, weight_grad)


def solution(mesh):
    in_specs = (
        P("pb", None, None),
        P("ctx", None),
        P(None, "pb", None),
        P("ctx", None),
        P("pb", None),
        P("pb"),
        P("pb"),
    )
    out_specs = (P("pb"), P("ctx", None), P("ctx", "pb", None), P("pb", None))
    return jax.shard_map(local, mesh=mesh, in_specs=in_specs, out_specs=out_specs, check_vma=False)
```

profile of v0, /device:TPU:0, one launch (start us, length us, event | category | flops | bytes accessed | tf_op | source)
XLA Modules:
  0.0 962.7 jit_solution(8131822947515228841)
XLA Ops:
  7.3 26.7 %copy.14 = bf16[128,128,576]{0,2,1:T(8,128)(2,1)} copy(bf16[128,128,576]{1,2,0:T(8,128)(2,1)} %param.11) | data formatting | bytes 37748736
  34.0 74.6 %while.29 = (s32[]{:T(128)}, f32[8,128,16]{1,2,0:T(8,128)S(1)}, f32[8,128,16]{1,2,0:T(8,128)S(1)}, f32[8,128,16,512]{3,1,2,0:T(8,128)}, s32[8]{0:T(128)S(1)}, /*...) while((s32[]{:T(128)}, f32[8,128,16]{1,2,0:T(8,128)S(1)}, ...), condition=%wide.region_3.4_spmd.clone, body=%wide.region_0.3_spmd.clone.sunk | while | flops 1220734976 | bytes 20057800 | solution.py:40
  82.0 3.8 fusion.30
  91.3 3.8 fusion.30
  100.7 3.8 fusion.30
  109.3 7.0 multiply_reduce_fusion.1
  116.8 84.4 %pmax.15 = f32[128]{0:T(128)S(1)} all-reduce(f32[128]{0:T(128)S(1)} %fusion.15), channel_id=1, replica_groups=mesh['ctx'=32,'pb'=4] {'ctx'}, use_global_device_ids=true, to_apply=%region_11.12 | all-reduce | flops 128 | bytes 1024 | tf_op jit(solution)/shard_map/pmax | solution.py:52
  201.1 181.7 %all-reduce.5.cloned.1.call-done = f32[128,128]{0,1:T(8,128)} async-done(((f32[128,128]{0,1:T(8,128)}), f32[128,128]{0,1:T(8,128)}) %all-reduce.5.cloned.1.call-update) | async-done | bytes 65552 | tf_op jit(solution)/shard_map/pmax | solution.py:52
  384.4 80.1 %psum.36 = f32[128]{0:T(128)S(1)} all-reduce(f32[128]{0:T(128)S(1)} %exponential_multiply_fusion), channel_id=1, replica_groups=mesh['ctx'=32,'pb'=4] {'ctx'}, use_global_device_ids=true, to_apply=%region_13.14 | all-reduce | flops 128 | bytes 1024 | tf_op jit(solution)/shard_map/psum | solution.py:53
  464.5 189.7 %all-reduce.7.cloned.1.call-done = f32[128,128]{0,1:T(8,128)} async-done(((f32[128,128]{0,1:T(8,128)}), f32[128,128]{0,1:T(8,128)}) %all-reduce.7.cloned.1.call-update) | async-done | bytes 65552 | tf_op jit(solution)/shard_map/psum | solution.py:53
  655.1 80.4 %while.30 = (s32[]{:T(128)}, f32[128,512]{1,0:T(8,128)S(1)}, f32[8,128,16,512]{3,1,2,0:T(8,128)}, f32[8,128,16]{1,2,0:T(8,128)S(1)}, s32[]{:T(128)}, /*index=5*/s32[]{:T(128)}) while((s32[]{:T(128)}, f32[128,512]{1,0:T(8,128)S(1)}, f32[8,128,16,512]{3,1,2,0:T(8,128)}, f32[8,128,16]{1,2,0:T(8,128)S(1)}, s32[]{:T(128)}, ...), condition=%wide.region_8.9_spmd.clone, body=%wide.region_6.8_spmd.clone.sunk | while | flops 2162691 | bytes 13672535 | solution.py:71
  655.1 4.8 constant_dynamic-slice_fusion.4
  660.1 5.0 fusion.32
  665.2 4.8 constant_dynamic-slice_fusion.4
  670.1 5.0 fusion.32
  675.2 4.8 constant_dynamic-slice_fusion.4
  680.2 5.0 fusion.32
  685.3 4.8 constant_dynamic-slice_fusion.4
  690.2 5.0 fusion.32
  695.3 4.8 constant_dynamic-slice_fusion.4
  700.3 5.0 fusion.32
  705.4 4.8 constant_dynamic-slice_fusion.4
  710.3 5.0 fusion.32
  715.4 4.8 constant_dynamic-slice_fusion.4
  720.4 5.0 fusion.32
  725.5 4.8 constant_dynamic-slice_fusion.4
  730.4 5.0 fusion.32
  735.9 9.1 convolution_bitcast_fusion
  745.0 8.5 fusion.16
  753.6 7.6 multiply_reduce_fusion
  761.2 155.3 %all-reduce = (f32[128]{0:T(128)}, f32[128,64]{0,1:T(8,128)}) all-reduce(f32[128]{0:T(128)S(1)} %get-tuple-element.234, f32[128,64]{0,1:T(8,128)S(1)} %multiply_bitcast_fusion), channel_id=1, replica_groups=mesh['ctx'=32,'pb'=4] {'ctx'}, use_global_device_ids=true, to_apply=%region_15.16 | all-reduce | flops 8320 | bytes 66560 | tf_op jit(solution)/shard_map/psum | solution.py:88
  916.5 38.0 %reduce-scatter.2.cloned.1.call-done = f32[2,128,128]{2,1,0:T(8,128)} async-done(((f32[64,128,128]{2,1,0:T(8,128)}), f32[2,128,128]{2,1,0:T(8,128)}) %reduce-scatter.2.cloned.1.call-update) | async-done | bytes 131088 | tf_op jit(solution)/shard_map/reduce_scatter | solution.py:92
  (110 shorter events, 65.1 us)
Async XLA Ops:
  7.2 102.1 %copy-start = (bf16[64,128,128]{2,1,0:T(8,128)(2,1)S(1)}, bf16[64,128,128]{2,1,0:T(8,128)(2,1)}, u32[]{:S(2)}) copy-start(bf16[64,128,128]{2,1,0:T(8,128)(2,1)} %param.13) | copy-start | bytes 6291460
  7.2 375.6 %all-reduce.5.cloned.1.call-start = ((), (), s32[]{:S(2)}) async-start(), calls=%async_computation.1 | async-start | bytes 131072 | tf_op jit(solution)/shard_map/pmax | solution.py:52
  7.3 26.7 %copy-start.6 = (s32[128]{0:T(128)S(1)}, s32[128]{0:T(128)}, u32[]{:S(2)}) copy-start(s32[128]{0:T(128)} %param.16) | copy-start | bytes 1540
  7.3 26.7 %copy-start.7 = (s32[128]{0:T(128)S(1)}, s32[128]{0:T(128)}, u32[]{:S(2)}) copy-start(s32[128]{0:T(128)} %param.17) | copy-start | bytes 1540
  7.3 26.7 %copy-start.1 = (bf16[512,576]{0,1:T(8,128)(2,1)S(1)}, bf16[512,576]{0,1:T(8,128)(2,1)}, u32[]{:S(2)}) copy-start(bf16[512,576]{0,1:T(8,128)(2,1)} %param.12) | copy-start | bytes 1769476
  34.0 75.3 %copy-start.4 = (bf16[512,128]{1,0:T(8,128)(2,1)S(1)}, bf16[512,128]{1,0:T(8,128)(2,1)}, u32[]{:S(2)}) copy-start(bf16[512,128]{1,0:T(8,128)(2,1)} %param.14) | copy-start | bytes 393220
  34.0 75.3 %copy-start.5 = (f32[128,64]{0,1:T(8,128)S(1)}, f32[128,64]{0,1:T(8,128)}, u32[]{:S(2)}) copy-start(f32[128,64]{0,1:T(8,128)} %param.15) | copy-start | bytes 98308
  108.6 0.6 copy-start.2
  109.3 545.0 %all-reduce.7.cloned.1.call-start = ((), (), s32[]{:S(2)}) async-start(), calls=%async_computation.2 | async-start | bytes 131072 | tf_op jit(solution)/shard_map/psum | solution.py:53
  109.3 273.4 %copy-start.3 = (f32[8,128,16]{1,2,0:T(8,128)S(1)}, f32[8,128,16]{1,2,0:T(8,128)}, u32[]{:S(2)}) copy-start(f32[8,128,16]{1,2,0:T(8,128)} %copy-done.2) | copy-start | bytes 196612
  384.3 532.2 %all-reduce.9.cloned.1.call-start = ((), (), s32[]{:S(2)}) async-start(), calls=%async_computation.3 | async-start | bytes 524288 | tf_op jit(solution)/shard_map/psum | solution.py:98
  745.0 209.5 %reduce-scatter.2.cloned.1.call-start = ((), (), s32[]{:S(2)}) async-start(), calls=%async_computation.4 | async-start | bytes 4325376 | tf_op jit(solution)/shard_map/reduce_scatter | solution.py:92
Sparse Core Ops, SparseCore 0:
  109.4 273.3 all-reduce.4
  386.0 268.2 all-reduce.6
  745.1 38.2 all-reduce.8
  786.4 168.0 reduce-scatter.1
where the time goes:
time: 965 us; the launch traced here: 963 us
  waiting for transfers between devices  410 us (42%)
  blocking collectives  320 us (33%)
  other arithmetic  85.6 us (9%)
  local copies, waits for them, and re-layouts  73.3 us (8%)
  matrix products  54.6 us (6%)
  between operations  14 us (1%)
    psum x1, waiting for transfers between devices, local(): lax.psum((main_total * jnp.exp(main_peak - global_main), index_total * jn...  190 us
    pmax x1, waiting for transfers between devices, local(): global_main, global_index = lax.pmax((main_peak, index_peak), 'ctx')  182 us
    psum x1, blocking collectives, local(): kl_loss, weight_grad = lax.psum((loss_local, weight_local), 'ctx')  155 us
    pmax x1, blocking collectives, local(): global_main, global_index = lax.pmax((main_peak, index_peak), 'ctx')  84.4 us
    psum x1, blocking collectives, local(): lax.psum((main_total * jnp.exp(main_peak - global_main), index_total * jn...  80.1 us
    reduce_sum x8, other arithmetic, add_kept(): jnp.sum(kept[group_id] * factor[group_id][:, :, None], axis=1)  39.9 us
    dynamic_slice x8, local copies, waits for them, and re-layouts, add_kept(): kept[group_id] * factor[group_id][:, :, None]  38.6 us
    reduce_scatter x1, waiting for transfers between devices, local(): lax.psum_scatter(jnp.einsum('jqt,td->jqd', coefficient, index_keys, prefe...  38 us
  transfers between devices with their start and end apart: 4, of which 3 were waited for; matrix products, arithmetic and copies ran while one was open for 2% of the time, Pallas kernels for 0%

commit v1 on v0

v1 whole, which is shorter than its diff:
```python
import functools
import math

import jax
import jax.numpy as jnp
from jax import lax
from jax.experimental import pallas as pl
from jax.experimental.pallas import tpu as pltpu
from jax.sharding import PartitionSpec as P

NEG = -1e30
LOG2E = math.log2(math.e)
MESH = pl.DeviceIdType.MESH
F32 = jnp.float32
BF16 = jnp.bfloat16
ZGROUP = 4
QBLOCK = 8


def nt_dot(lhs, rhs):
    return lax.dot_general(lhs, rhs, (((1,), (1,)), ((), ())), preferred_element_type=F32)


def nn_dot(lhs, rhs):
    return jnp.dot(lhs, rhs, preferred_element_type=F32)


def wait_bytes(ref, sem):
    pltpu.make_async_copy(ref, ref, sem).wait()


def kernel(
    n_ctx, n_pb, loss_scale,
    q_hbm, kt_ref, iq_ref, ik_ref, wt_ref, pos_ref, len_ref,
    kl_ref, key_ref, qg_ref, wg_ref,
    qb, ke, s_ref, p_ref, logit_ref, dl_ref, fac_ref, fact_hi, fact_lo, f_ref, tacc,
    ikt_all, ik_all, coef, coef2,
    key_send, key_gather, dl_gather,
    ist_send, ist_recv, st_send, st_recv, lse_send, lse_recv,
    kp_ref, kp_recv, ko_ref, t_send, t_recv, w_send, w_recv, qs_ref, q_recv,
    q_sem, send_sem, recv_sem, zk_sem, zd_sem,
):
    ctx = lax.axis_index("ctx")
    pb = lax.axis_index("pb")
    z = lax.rem(ctx, ZGROUP)
    grp = ctx // ZGROUP
    n_grp = n_ctx // ZGROUP
    heads = iq_ref.shape[0]
    pairs = heads // 2
    queries, lat, lanes = q_hbm.shape
    t_rows = ik_ref.shape[0]
    idim = ik_ref.shape[1]
    blocks = queries // QBLOCK
    iscale = idim ** -0.5
    mscale = 192 ** -0.5 * LOG2E

    def ctx_peer(r):
        return lax.rem(ctx + r, n_ctx)

    def pb_peer(r):
        return lax.rem(pb + r, n_pb)

    def z_peer(r):
        return grp * ZGROUP + lax.rem(z + r, ZGROUP)

    barrier = pltpu.get_barrier_semaphore()

    @pl.loop(1, n_ctx)
    def _(r):
        pl.semaphore_signal(barrier, inc=1, device_id=(ctx_peer(r), pb), device_id_type=MESH)

    @pl.loop(1, n_pb)
    def _(r):
        pl.semaphore_signal(barrier, inc=1, device_id=(ctx, pb_peer(r)), device_id_type=MESH)

    def q_copy(block, slot):
        return pltpu.make_async_copy(
            q_hbm.at[pl.ds(block * QBLOCK, QBLOCK)],
            qb.at[slot, :, pl.ds(lanes, lat), :],
            q_sem.at[slot],
        )

    q_copy(0, 0).start()
    q_copy(1, 1).start()

    t_index = ctx * t_rows + lax.broadcasted_iota(jnp.int32, (t_rows, lanes), 0)
    pos = pos_ref[...]
    visible = (t_index <= pos) & (t_index > pos - len_ref[...])
    bias = jnp.where(visible, 0.0, NEG)
    ke[:, 0:lanes] = bias.astype(BF16)
    ke[:, lanes:lanes + lat] = kt_ref[...].astype(F32).T.astype(BF16)
    depth = ke.shape[1]
    pad = depth - lanes - lat
    ke[:, lanes + lat:] = jnp.zeros((t_rows, pad), BF16)
    for slot in range(2):
        for i in range(QBLOCK):
            qb[slot, i, lanes + lat:, :] = jnp.zeros((pad, lanes), BF16)

    ik = ik_ref[...]
    key_send[...] = ik.astype(F32)

    logit_ref[...] = jnp.zeros_like(logit_ref)

    @pl.loop(0, pairs // 4)
    def _(step):
        total = logit_ref[...]
        for u in range(4):
            jp = step * 4 + u
            raw = nt_dot(ik, iq_ref[pl.ds(2 * jp, 2)].reshape(2 * lanes, idim))
            w = wt_ref[pl.ds(2 * jp, 2), :]
            total = total + jnp.maximum(raw[:, :lanes], 0.0) * w[0:1]
            total = total + jnp.maximum(raw[:, lanes:], 0.0) * w[1:2]
        logit_ref[...] = total

    logits = logit_ref[...] * (iscale * LOG2E) + bias
    logit_ref[...] = logits
    i_peak = jnp.max(logits, axis=0, keepdims=True)
    i_sum = jnp.sum(jnp.exp2(logits - i_peak), axis=0, keepdims=True)
    ist_send[...] = jnp.zeros_like(ist_send)
    ist_send[0:1, :] = i_peak
    ist_send[1:2, :] = i_sum

    pl.semaphore_wait(barrier, n_ctx - 1 + n_pb - 1)

    for r in range(1, ZGROUP):
        pltpu.make_async_remote_copy(
            key_send, key_gather.at[r - 1], send_sem.at[0], zk_sem.at[r - 1],
            device_id=(z_peer(r), pb), device_id_type=MESH,
        ).start()

    @pl.loop(1, n_ctx)
    def _(r):
        pltpu.make_async_remote_copy(
            ist_send, ist_recv.at[r - 1], send_sem.at[1], recv_sem.at[1],
            device_id=(ctx_peer(r), pb), device_id_type=MESH,
        ).start()

    @pl.loop(0, blocks)
    def _(block):
        slot = lax.rem(block, 2)
        q_copy(block, slot).wait()
        row = lax.broadcasted_iota(jnp.int32, (lanes, lanes), 0)
        for i in range(QBLOCK):
            qb[slot, i, 0:lanes, :] = jnp.where(row == block * QBLOCK + i, 1.0, 0.0).astype(BF16)
        for u in range(QBLOCK // 2):
            rhs = jnp.concatenate([qb[slot, 2 * u], qb[slot, 2 * u + 1]], axis=1)
            s_ref[u % 2] = nn_dot(ke[...], rhs)
            s = s_ref[u % 2]
            peak = jnp.max(s, axis=0, keepdims=True) * mscale
            expo = jnp.exp2(s * mscale - peak)
            total = jnp.sum(expo, axis=0, keepdims=True)
            p_ref[block, :, 2 * u * lanes:(2 * u + 2) * lanes] = expo.astype(BF16)
            for h in range(2):
                i = 2 * u + h
                owner = block * (QBLOCK // 4) + i // 4
                st_send[owner, pl.ds(i % 4, 1), :] = peak[:, h * lanes:(h + 1) * lanes]
                st_send[owner, pl.ds(4 + i % 4, 1), :] = total[:, h * lanes:(h + 1) * lanes]

        @pl.when(block + 2 < blocks)
        def _():
            q_copy(block + 2, slot).start()

    @pl.loop(1, n_ctx)
    def _(r):
        peer = ctx_peer(r)
        pltpu.make_async_remote_copy(
            st_send.at[peer], st_recv.at[r - 1], send_sem.at[2], recv_sem.at[2],
            device_id=(peer, pb), device_id_type=MESH,
        ).start()

    ik_all[0:t_rows, :] = ik
    ikt_all[:, 0:t_rows] = key_send[...].T.astype(BF16)
    for r in range(1, ZGROUP):
        wait_bytes(key_gather.at[r - 1], zk_sem.at[r - 1])
        got = key_gather[r - 1]
        ik_all[r * t_rows:(r + 1) * t_rows, :] = got.astype(BF16)
        ikt_all[:, r * t_rows:(r + 1) * t_rows] = got.T.astype(BF16)

    wait_bytes(ist_recv.at[pl.ds(0, n_ctx - 1)], recv_sem.at[1])
    ist_recv[n_ctx - 1] = ist_send[...]
    got = ist_recv[...]
    peaks, sums = got[:, 0:1, :], got[:, 1:2, :]
    top = jnp.max(peaks, axis=0)
    i_lse = top + jnp.log(jnp.sum(sums * jnp.exp2(peaks - top[None]), axis=0)) * LOG2E

    wait_bytes(st_recv.at[pl.ds(0, n_ctx - 1)], recv_sem.at[2])
    st_recv[n_ctx - 1] = st_send[ctx]
    got = st_recv[...]
    peaks, sums = got[:, 0:4, :], got[:, 4:8, :]
    top = jnp.max(peaks, axis=0)
    lse = top + jnp.log(jnp.sum(sums * jnp.exp2(peaks - top[None]), axis=0)) * LOG2E
    lse_send[...] = jnp.zeros_like(lse_send)
    lse_send[0:4, :] = lse

    @pl.loop(1, n_ctx)
    def _(r):
        pltpu.make_async_remote_copy(
            lse_send, lse_recv.at[ctx], send_sem.at[3], recv_sem.at[3],
            device_id=(ctx_peer(r), pb), device_id_type=MESH,
        ).start()

    tacc[...] = jnp.zeros_like(tacc)
    wait_bytes(lse_recv.at[pl.ds(0, n_ctx - 1)], recv_sem.at[3])
    lse_recv[ctx] = lse_send[...]
    for i in range(n_ctx):
        fac_ref[4 * i:4 * i + 4, :] = jnp.exp2(st_send[i, 0:4, :] - lse_recv[i, 0:4, :])
    fact = fac_ref[...].T * (1.0 / lanes)
    hi = fact.astype(BF16)
    fact_hi[...] = hi.astype(F32)
    fact_lo[...] = fact - hi.astype(F32)

    @pl.loop(0, blocks)
    def _(block):
        lane = lax.broadcasted_iota(jnp.int32, (lanes, lanes), 1)
        for i in range(QBLOCK):
            here = lane == block * QBLOCK + i
            f_ref[i * lanes:(i + 1) * lanes, 0:lanes] = jnp.where(here, fact_hi[...], 0.0).astype(BF16)
            f_ref[i * lanes:(i + 1) * lanes, lanes:] = jnp.where(here, fact_lo[...], 0.0).astype(BF16)
        tacc[...] += nn_dot(p_ref[block], f_ref[...])

    target = tacc[:, 0:lanes] + tacc[:, lanes:]
    log_index = logit_ref[...] - i_lse
    index_prob = jnp.exp2(log_index)
    positive = target > 0
    log_target = jnp.log(jnp.where(positive, target, 1.0))
    kl = jnp.sum(
        jnp.where(positive, target * (log_target - log_index * math.log(2.0)), 0.0), axis=0, keepdims=True
    )
    dl_ref[0] = loss_scale * (index_prob - target)

    for r in range(1, ZGROUP):
        pltpu.make_async_remote_copy(
            dl_ref.at[0], dl_gather.at[r - 1], send_sem.at[4], zd_sem.at[r - 1],
            device_id=(z_peer(r), pb), device_id_type=MESH,
        ).start()

    kp_ref[...] = jnp.zeros_like(kp_ref)

    @pl.loop(0, pairs // 4)
    def _(step):
        dl = dl_ref[0]
        for u in range(4):
            jp = step * 4 + u
            raw = nt_dot(ik, iq_ref[pl.ds(2 * jp, 2)].reshape(2 * lanes, idim))
            w = wt_ref[pl.ds(2 * jp, 2), :] * iscale
            for h in range(2):
                part = raw[:, h * lanes:(h + 1) * lanes]
                t_send[jp, pl.ds(h, 1), :] = (
                    jnp.sum(dl * jnp.maximum(part, 0.0), axis=0, keepdims=True) * iscale
                )
                coef[:, (2 * u + h) * lanes:(2 * u + h + 1) * lanes] = jnp.where(
                    part > 0, dl * w[h:h + 1], 0.0
                ).astype(BF16)
            t_send[jp, pl.ds(2, 1), :] = kl
            t_send[jp, pl.ds(3, 5), :] = jnp.zeros((5, lanes), F32)
        kp_ref[...] += nn_dot(coef[...], iq_ref[pl.ds(8 * step, 8)].reshape(8 * lanes, idim))

    @pl.loop(1, n_ctx)
    def _(r):
        peer = ctx_peer(r)
        pltpu.make_async_remote_copy(
            t_send.at[peer], t_recv.at[r - 1], send_sem.at[5], recv_sem.at[5],
            device_id=(peer, pb), device_id_type=MESH,
        ).start()

    q_rows = t_rows // n_pb
    for r in range(1, n_pb):
        peer = pb_peer(r)
        pltpu.make_async_remote_copy(
            kp_ref.at[pl.ds(peer * q_rows, q_rows)], kp_recv.at[r - 1], send_sem.at[6], recv_sem.at[6],
            device_id=(ctx, peer), device_id_type=MESH,
        ).start()

    for r in range(1, ZGROUP):
        wait_bytes(dl_gather.at[r - 1], zd_sem.at[r - 1])
        dl_ref[r] = dl_gather[r - 1]

    def query_pair(step):
        k = lax.rem(grp + 1 + step, n_grp)
        jp = k * ZGROUP + z
        iq_pair = iq_ref[pl.ds(2 * jp, 2)].reshape(2 * lanes, idim)
        w = wt_ref[pl.ds(2 * jp, 2), :] * iscale
        for r in range(ZGROUP):
            raw = nt_dot(ik_all[r * t_rows:(r + 1) * t_rows, :], iq_pair)
            dl = dl_ref[r]
            for h in range(2):
                coef2[r * t_rows:(r + 1) * t_rows, h * lanes:(h + 1) * lanes] = jnp.where(
                    raw[:, h * lanes:(h + 1) * lanes] > 0, dl * w[h:h + 1], 0.0
                ).astype(BF16)
        grad = nn_dot(ikt_all[...], coef2[...])
        for h in range(2):
            qs_ref[step, h] = grad[:, h * lanes:(h + 1) * lanes]
        return k

    @pl.loop(0, n_grp - 1)
    def _(step):
        k = query_pair(step)
        pltpu.make_async_remote_copy(
            qs_ref.at[step], q_recv.at[step], send_sem.at[7], recv_sem.at[7],
            device_id=(k * ZGROUP + z, pb), device_id_type=MESH,
        ).start()

    wait_bytes(kp_recv, recv_sem.at[6])
    own_quarter = kp_ref[pl.ds(pb * q_rows, q_rows), :] + kp_recv[0] + kp_recv[1] + kp_recv[2]
    ko_ref[pb] = own_quarter
    for r in range(1, n_pb):
        pltpu.make_async_remote_copy(
            ko_ref.at[pb], ko_ref.at[pb], send_sem.at[8], recv_sem.at[8],
            device_id=(ctx, pb_peer(r)), device_id_type=MESH,
        ).start()

    wait_bytes(t_recv.at[pl.ds(0, n_ctx - 1)], recv_sem.at[5])
    w_total = jnp.sum(t_recv[0:n_ctx - 1], axis=0) + t_send[ctx]
    w_send[...] = w_total
    kl_ref[...] = w_total[2:3, :]

    @pl.loop(1, n_ctx)
    def _(r):
        pltpu.make_async_remote_copy(
            w_send, w_recv.at[ctx], send_sem.at[9], recv_sem.at[9],
            device_id=(ctx_peer(r), pb), device_id_type=MESH,
        ).start()

    query_pair(n_grp - 1)

    wait_bytes(ko_ref.at[pl.ds(0, n_pb - 1)], recv_sem.at[8])
    for i in range(n_pb):
        key_ref[i * q_rows:(i + 1) * q_rows, :] = ko_ref[i]
    wait_bytes(w_recv.at[pl.ds(0, n_ctx - 1)], recv_sem.at[9])
    w_recv[ctx] = w_send[...]
    for i in range(n_ctx):
        wg_ref[2 * i:2 * i + 2, :] = w_recv[i, 0:2, :]

    wait_bytes(q_recv, recv_sem.at[7])
    for h in range(2):
        total = qs_ref[n_grp - 1, h]
        for k in range(n_grp - 1):
            total = total + q_recv[k, h]
        qg_ref[h] = total.T

    wait_bytes(key_gather, send_sem.at[0])
    wait_bytes(ist_recv.at[pl.ds(0, n_ctx - 1)], send_sem.at[1])
    wait_bytes(st_recv.at[pl.ds(0, n_ctx - 1)], send_sem.at[2])
    wait_bytes(lse_recv.at[pl.ds(0, n_ctx - 1)], send_sem.at[3])
    wait_bytes(dl_gather, send_sem.at[4])
    wait_bytes(t_recv.at[pl.ds(0, n_ctx - 1)], send_sem.at[5])
    wait_bytes(kp_recv, send_sem.at[6])
    wait_bytes(q_recv, send_sem.at[7])
    wait_bytes(ko_ref.at[pl.ds(0, n_pb - 1)], send_sem.at[8])
    wait_bytes(w_recv.at[pl.ds(0, n_ctx - 1)], send_sem.at[9])


def local(queries, key_cache, index_queries, index_keys, head_weights, positions, valid_lengths):
    n_ctx, n_pb = lax.axis_size("ctx"), lax.axis_size("pb")
    q_rows, lanes, lat = queries.shape
    t_rows, idim = index_keys.shape
    heads = index_queries.shape[0]
    blocks = q_rows // QBLOCK
    n_grp = n_ctx // ZGROUP
    depth = -(-(lanes + lat) // 256) * 256
    loss_scale = t_rows * n_ctx / (q_rows * n_pb)
    vmem = pltpu.VMEM
    tile = (8, lanes)
    scratch = [
        vmem((2, QBLOCK, depth, lanes), BF16),
        vmem((t_rows, depth), BF16),
        vmem((2, t_rows, 2 * lanes), F32),
        vmem((blocks, t_rows, QBLOCK * lanes), BF16),
        vmem((t_rows, lanes), F32),
        vmem((ZGROUP, t_rows, lanes), F32),
        vmem((q_rows, lanes), F32),
        vmem((lanes, q_rows), F32),
        vmem((lanes, q_rows), F32),
        vmem((QBLOCK * lanes, 2 * lanes), BF16),
        vmem((t_rows, 2 * lanes), F32),
        vmem((idim, ZGROUP * t_rows), BF16),
        vmem((ZGROUP * t_rows, idim), BF16),
        vmem((t_rows, 8 * lanes), BF16),
        vmem((ZGROUP * t_rows, 2 * lanes), BF16),
        vmem((t_rows, idim), F32),
        vmem((ZGROUP - 1, t_rows, idim), F32),
        vmem((ZGROUP - 1, t_rows, lanes), F32),
        vmem(tile, F32),
        vmem((n_ctx, *tile), F32),
        vmem((n_ctx, *tile), F32),
        vmem((n_ctx, *tile), F32),
        vmem(tile, F32),
        vmem((n_ctx, *tile), F32),
        vmem((t_rows, idim), F32),
        vmem((n_pb - 1, t_rows // n_pb, idim), F32),
        vmem((n_pb, t_rows // n_pb, idim), F32),
        vmem((n_ctx, *tile), F32),
        vmem((n_ctx, *tile), F32),
        vmem(tile, F32),
        vmem((n_ctx, *tile), F32),
        vmem((n_grp, 2, idim, lanes), F32),
        vmem((n_grp - 1, 2, idim, lanes), F32),
        pltpu.SemaphoreType.DMA((2,)),
        pltpu.SemaphoreType.DMA((10,)),
        pltpu.SemaphoreType.DMA((10,)),
        pltpu.SemaphoreType.DMA((ZGROUP - 1,)),
        pltpu.SemaphoreType.DMA((ZGROUP - 1,)),
    ]
    on_chip = pl.BlockSpec(memory_space=pltpu.VMEM)
    kl, key_grad, query_grad, weight_grad = pl.pallas_call(
        functools.partial(kernel, n_ctx, n_pb, loss_scale),
        out_shape=(
            jax.ShapeDtypeStruct((1, q_rows), F32),
            jax.ShapeDtypeStruct((t_rows, idim), F32),
            jax.ShapeDtypeStruct((heads // n_ctx, q_rows, idim), F32),
            jax.ShapeDtypeStruct((heads, q_rows), F32),
        ),
        in_specs=[pl.BlockSpec(memory_space=pl.ANY)] + [on_chip] * 6,
        out_specs=(on_chip,) * 4,
        scratch_shapes=scratch,
        compiler_params=pltpu.CompilerParams(
            collective_id=0, has_side_effects=True, vmem_limit_bytes=60 * 1024 * 1024
        ),
    )(
        queries.transpose(0, 2, 1),
        key_cache.T,
        index_queries,
        index_keys,
        head_weights.T,
        positions.reshape(1, q_rows),
        valid_lengths.reshape(1, q_rows),
    )
    return kl.reshape(q_rows), key_grad, query_grad, weight_grad.T


def solution(mesh):
    in_specs = (
        P("pb", None, None),
        P("ctx", None),
        P(None, "pb", None),
        P("ctx", None),
        P("pb", None),
        P("pb"),
        P("pb"),
    )
    out_specs = (P("pb"), P("ctx", None), P("ctx", "pb", None), P("pb", None))
    return jax.shard_map(local, mesh=mesh, in_specs=in_specs, out_specs=out_specs, check_vma=False)
```

time: 965 us -> 94.9 us (0.10)
  waiting for transfers between devices: 410 us -> 0 us
  blocking collectives: 320 us -> 0 us
  Pallas kernels: 0 us -> 88.2 us
  other arithmetic: 85.6 us -> 0 us
  local copies, waits for them, and re-layouts: 73.3 us -> 5.73 us
  matrix products: 54.6 us -> 0 us
  between operations: 14 us -> 0.64 us
    psum x2 -> x0, blocking collectives: 235 us -> none  [the longest x1 155 us: local(): kl_loss, weight_grad = lax.psum((loss_local, weight_local), 'ctx')]
    psum x2 -> x0, waiting for transfers between devices: 190 us -> none  [the longest x1 190 us: local(): lax.psum((main_total * jnp.exp(main_peak - global_main), index_total * jn...]
    pmax x1 -> x0, waiting for transfers between devices: 182 us -> none  [local(): global_main, global_index = lax.pmax((main_peak, index_peak), 'ctx')]
    pallas_call x0 -> x1, Pallas kernels: none -> 88.2 us  [local(): pl.pallas_call(functools.partial(kernel, n_ctx, n_pb, loss_scale), out_sh...]
    pmax x1 -> x0, blocking collectives: 84.4 us -> none  [local(): global_main, global_index = lax.pmax((main_peak, index_peak), 'ctx')]
    reduce_sum x18 -> x0, other arithmetic: 58 us -> none  [the longest x8 39.9 us: add_kept(): jnp.sum(kept[group_id] * factor[group_id][:, :, None], axis=1)]
    dot_general x11 -> x0, matrix products: 54.6 us -> none  [the longest x8 30.1 us: group_scores(): jnp.einsum('qhc,tc->qht', query_block, key_cache, preferred_element_type=...]
    dynamic_slice x32 -> x0, local copies, waits for them, and re-layouts: 44.2 us -> none  [the longest x8 38.6 us: add_kept(): kept[group_id] * factor[group_id][:, :, None]]
  transfers between devices with their start and end apart: 4 -> 0, of which waited for: 3 -> 0; matrix products, arithmetic and copies ran while one was open for 2% -> 0% of each run, Pallas kernels for 0% -> 0%
where the time goes in v1:
time: 94.9 us; the launch traced here: 94.6 us
  Pallas kernels  88.2 us (93%)
  local copies, waits for them, and re-layouts  5.73 us (6%)
    pallas_call x1, Pallas kernels, local(): pl.pallas_call(functools.partial(kernel, n_ctx, n_pb, loss_scale), out_sh...  88.2 us
    unnamed x4, local copies, waits for them, and re-layouts  5.73 us

profile of v1, /device:TPU:0, one launch (start us, length us, event | category | flops | bytes accessed | tf_op | source)
XLA Modules:
  0.0 94.6 jit_solution(195569863674777753)
XLA Ops:
  0.6 88.2 %shard_map.102 = (f32[1,128]{1,0:T(1,128)}, f32[512,128]{1,0:T(8,128)}, f32[2,128,128]{2,1,0:T(8,128)}, f32[64,128]{1,0:T(8,128)}) custom-call(bf16[128,576,128]{2,1,0:T(8,128)(2,1)} %bitcast.7, bf16[576,512]{1,0:T(8,128)(2,1)} %bitcast.8, bf16[64,128,128]{2,1,0:T(8,128)(2,1)} %iq_ref.1, bf16[512,128]{1,0:T(8,128)(2,1)} %ik_ref.1, f32[64,128]{1,0:T(8,128)} %bitcast.9, ...), custom_call_target="tpu_custom_call" | custom-call | tf_op jit(solution)/shard_map/pallas_call | solution.py:405
  88.9 1.1 %copy.15 = f32[128]{0:T(128)} copy(f32[128]{0:T(128)} %bitcast.13) | data formatting | bytes 1024
  90.0 1.7 %copy.16 = f32[512,128]{1,0:T(8,128)} copy(f32[512,128]{1,0:T(8,128)} %get-tuple-element.17) | data formatting | bytes 524288
  91.7 1.6 %copy.17 = f32[2,128,128]{2,1,0:T(8,128)} copy(f32[2,128,128]{2,1,0:T(8,128)} %get-tuple-element.18) | data formatting | bytes 262144
  93.2 1.4 %copy.18 = f32[128,64]{0,1:T(8,128)} copy(f32[128,64]{0,1:T(8,128)} %bitcast.10) | data formatting | bytes 65536

commit v2 on v1

--- a/solution.py
+++ b/solution.py
@@ -15,6 +15,8 @@
 BF16 = jnp.bfloat16
 ZGROUP = 4
 QBLOCK = 8
+OWNED = 4
+FIRST = 3
 
 
 def nt_dot(lhs, rhs):
@@ -31,14 +33,15 @@
 
 def kernel(
     n_ctx, n_pb, loss_scale,
-    q_hbm, kt_ref, iq_ref, ik_ref, wt_ref, pos_ref, len_ref,
+    q_hbm, kt_ref, iq_hbm, ik_ref, wt_ref, pos_ref, len_ref,
     kl_ref, key_ref, qg_ref, wg_ref,
-    qb, ke, s_ref, p_ref, logit_ref, dl_ref, fac_ref, fact_hi, fact_lo, f_ref, tacc,
+    iq_ref, qb, ke, s_ref, peak_ref, p_ref, logit_ref, dl_ref, fac_ref, fact_hi, fact_lo, f_ref, tacc,
     ikt_all, ik_all, coef, coef2,
     key_send, key_gather, dl_gather,
     ist_send, ist_recv, st_send, st_recv, lse_send, lse_recv,
     kp_ref, kp_recv, ko_ref, t_send, t_recv, w_send, w_recv, qs_ref, q_recv,
-    q_sem, send_sem, recv_sem, zk_sem, zd_sem,
+    iq_sem, q_sem, send_sem, recv_sem, zk_sem, zd_sem,
+    st_ssem, st_rsem, lse_ssem, lse_rsem,
 ):
     ctx = lax.axis_index("ctx")
     pb = lax.axis_index("pb")
@@ -47,7 +50,8 @@
     n_grp = n_ctx // ZGROUP
     heads = iq_ref.shape[0]
     pairs = heads // 2
-    queries, lat, lanes = q_hbm.shape
+    _, _, lat, lanes = q_hbm.shape
+    queries = OWNED * n_ctx
     t_rows = ik_ref.shape[0]
     idim = ik_ref.shape[1]
     blocks = queries // QBLOCK
@@ -73,15 +77,22 @@
     def _(r):
         pl.semaphore_signal(barrier, inc=1, device_id=(ctx, pb_peer(r)), device_id_type=MESH)
 
+    per_row = n_ctx // QBLOCK
+
+    def first_query(block):
+        return OWNED * QBLOCK * lax.rem(block, per_row) + block // per_row
+
     def q_copy(block, slot):
         return pltpu.make_async_copy(
-            q_hbm.at[pl.ds(block * QBLOCK, QBLOCK)],
+            q_hbm.at[pl.ds(QBLOCK * lax.rem(block, per_row), QBLOCK), block // per_row],
             qb.at[slot, :, pl.ds(lanes, lat), :],
             q_sem.at[slot],
         )
 
     q_copy(0, 0).start()
     q_copy(1, 1).start()
+    iq_copy = pltpu.make_async_copy(iq_hbm, iq_ref, iq_sem)
+    iq_copy.start()
 
     t_index = ctx * t_rows + lax.broadcasted_iota(jnp.int32, (t_rows, lanes), 0)
     pos = pos_ref[...]
@@ -99,6 +110,103 @@
     ik = ik_ref[...]
     key_send[...] = ik.astype(F32)
 
+    pl.semaphore_wait(barrier, n_ctx - 1 + n_pb - 1)
+
+    for r in range(1, ZGROUP):
+        pltpu.make_async_remote_copy(
+            key_send, key_gather.at[r - 1], send_sem.at[0], zk_sem.at[r - 1],
+            device_id=(z_peer(r), pb), device_id_type=MESH,
+        ).start()
+
+    st_send[...] = jnp.zeros_like(st_send)
+
+    def exponentials(block):
+        row = block // per_row
+        part = row // FIRST
+        for u in range(QBLOCK // 2):
+            peak = peak_ref[u:u + 1, :]
+            expo = jnp.exp2(s_ref[:, 2 * u * lanes:(2 * u + 2) * lanes] * mscale - peak)
+            total = jnp.sum(expo, axis=0, keepdims=True)
+            p_ref[block, :, 2 * u * lanes:(2 * u + 2) * lanes] = expo.astype(BF16)
+            for h in range(2):
+                owner = QBLOCK * lax.rem(block, per_row) + 2 * u + h
+                st_send[part, owner, pl.ds(row, 1), :] = peak[:, h * lanes:(h + 1) * lanes]
+                st_send[part, owner, pl.ds(OWNED + row, 1), :] = total[:, h * lanes:(h + 1) * lanes]
+
+    def scores(block):
+        slot = lax.rem(block, 2)
+        q_copy(block, slot).wait()
+        row = lax.broadcasted_iota(jnp.int32, (lanes, lanes), 0)
+        first = first_query(block)
+        for i in range(QBLOCK):
+            qb[slot, i, 0:lanes, :] = jnp.where(row == first + OWNED * i, 1.0, 0.0).astype(BF16)
+        exponentials(lax.max(block - 1, 0))
+        rhs = jnp.concatenate([qb[slot, i] for i in range(QBLOCK)], axis=1)
+        s = nn_dot(ke[...], rhs)
+        s_ref[...] = s
+        peak = jnp.max(s, axis=0, keepdims=True) * mscale
+        for u in range(QBLOCK // 2):
+            peak_ref[u:u + 1, :] = peak[:, 2 * u * lanes:(2 * u + 2) * lanes]
+
+        @pl.when(block + 2 < blocks)
+        def _():
+            q_copy(block + 2, slot).start()
+
+    def send_stats(part):
+        @pl.loop(1, n_ctx)
+        def _(r):
+            peer = ctx_peer(r)
+            pltpu.make_async_remote_copy(
+                st_send.at[part, peer], st_recv.at[part, r - 1], st_ssem.at[part], st_rsem.at[part],
+                device_id=(peer, pb), device_id_type=MESH,
+            ).start()
+
+    def combine(part):
+        wait_bytes(st_recv.at[part, pl.ds(0, n_ctx - 1)], st_rsem.at[part])
+        st_recv[part, n_ctx - 1] = st_send[part, ctx]
+        got = st_recv[part]
+        peaks, sums = got[:, 0:OWNED, :], got[:, OWNED:, :]
+        top = jnp.max(peaks, axis=0)
+        total = jnp.sum(sums * jnp.exp2(peaks - top[None]), axis=0)
+        lse_send[part] = jnp.zeros((2 * OWNED, lanes), F32)
+        lse_send[part, 0:OWNED, :] = top + jnp.log(jnp.maximum(total, 1e-30)) * LOG2E
+
+        @pl.loop(1, n_ctx)
+        def _(r):
+            pltpu.make_async_remote_copy(
+                lse_send.at[part], lse_recv.at[part, ctx], lse_ssem.at[part], lse_rsem.at[part],
+                device_id=(ctx_peer(r), pb), device_id_type=MESH,
+            ).start()
+
+    def factors(part):
+        wait_bytes(lse_recv.at[part, pl.ds(0, n_ctx - 1)], lse_rsem.at[part])
+        lse_recv[part, ctx] = lse_send[part]
+        for i in range(n_ctx):
+            fac_ref[OWNED * i:OWNED * (i + 1), :] = jnp.exp2(
+                st_send[part, i, 0:OWNED, :] - lse_recv[part, i, 0:OWNED, :]
+            )
+        fact = fac_ref[...].T * (1.0 / lanes)
+        hi = fact.astype(BF16)
+        fact_hi[...] = hi.astype(F32)
+        fact_lo[...] = fact - hi.astype(F32)
+
+    split = FIRST * per_row
+
+    @pl.loop(0, split + 1)
+    def _(block):
+        scores(block)
+
+    send_stats(0)
+
+    @pl.loop(split + 1, blocks)
+    def _(block):
+        scores(block)
+
+    exponentials(blocks - 1)
+    send_stats(1)
+    combine(0)
+
+    iq_copy.wait()
     logit_ref[...] = jnp.zeros_like(logit_ref)
 
     @pl.loop(0, pairs // 4)
@@ -120,52 +228,11 @@
     ist_send[0:1, :] = i_peak
     ist_send[1:2, :] = i_sum
 
-    pl.semaphore_wait(barrier, n_ctx - 1 + n_pb - 1)
-
-    for r in range(1, ZGROUP):
-        pltpu.make_async_remote_copy(
-            key_send, key_gather.at[r - 1], send_sem.at[0], zk_sem.at[r - 1],
-            device_id=(z_peer(r), pb), device_id_type=MESH,
-        ).start()
-
     @pl.loop(1, n_ctx)
     def _(r):
         pltpu.make_async_remote_copy(
             ist_send, ist_recv.at[r - 1], send_sem.at[1], recv_sem.at[1],
             device_id=(ctx_peer(r), pb), device_id_type=MESH,
-        ).start()
-
-    @pl.loop(0, blocks)
-    def _(block):
-        slot = lax.rem(block, 2)
-        q_copy(block, slot).wait()
-        row = lax.broadcasted_iota(jnp.int32, (lanes, lanes), 0)
-        for i in range(QBLOCK):
-            qb[slot, i, 0:lanes, :] = jnp.where(row == block * QBLOCK + i, 1.0, 0.0).astype(BF16)
-        for u in range(QBLOCK // 2):
-            rhs = jnp.concatenate([qb[slot, 2 * u], qb[slot, 2 * u + 1]], axis=1)
-            s_ref[u % 2] = nn_dot(ke[...], rhs)
-            s = s_ref[u % 2]
-            peak = jnp.max(s, axis=0, keepdims=True) * mscale
-            expo = jnp.exp2(s * mscale - peak)
-            total = jnp.sum(expo, axis=0, keepdims=True)
-            p_ref[block, :, 2 * u * lanes:(2 * u + 2) * lanes] = expo.astype(BF16)
-            for h in range(2):
-                i = 2 * u + h
-                owner = block * (QBLOCK // 4) + i // 4
-                st_send[owner, pl.ds(i % 4, 1), :] = peak[:, h * lanes:(h + 1) * lanes]
-                st_send[owner, pl.ds(4 + i % 4, 1), :] = total[:, h * lanes:(h + 1) * lanes]
-
-        @pl.when(block + 2 < blocks)
-        def _():
-            q_copy(block + 2, slot).start()
-
-    @pl.loop(1, n_ctx)
-    def _(r):
-        peer = ctx_peer(r)
-        pltpu.make_async_remote_copy(
-            st_send.at[peer], st_recv.at[r - 1], send_sem.at[2], recv_sem.at[2],
-            device_id=(peer, pb), device_id_type=MESH,
         ).start()
 
     ik_all[0:t_rows, :] = ik
@@ -176,47 +243,36 @@
         ik_all[r * t_rows:(r + 1) * t_rows, :] = got.astype(BF16)
         ikt_all[:, r * t_rows:(r + 1) * t_rows] = got.T.astype(BF16)
 
+    combine(1)
+    tacc[...] = jnp.zeros_like(tacc)
+
+    def add_target(block):
+        lane = lax.broadcasted_iota(jnp.int32, (lanes, lanes), 1)
+        first = first_query(block)
+        for i in range(QBLOCK):
+            here = lane == first + OWNED * i
+            f_ref[i * lanes:(i + 1) * lanes, 0:lanes] = jnp.where(here, fact_hi[...], 0.0).astype(BF16)
+            f_ref[i * lanes:(i + 1) * lanes, lanes:] = jnp.where(here, fact_lo[...], 0.0).astype(BF16)
+        tacc[...] += nn_dot(p_ref[block], f_ref[...])
+
+    factors(0)
+
+    @pl.loop(0, split)
+    def _(block):
+        add_target(block)
+
+    factors(1)
+
+    @pl.loop(split, blocks)
+    def _(block):
+        add_target(block)
+
     wait_bytes(ist_recv.at[pl.ds(0, n_ctx - 1)], recv_sem.at[1])
     ist_recv[n_ctx - 1] = ist_send[...]
     got = ist_recv[...]
     peaks, sums = got[:, 0:1, :], got[:, 1:2, :]
     top = jnp.max(peaks, axis=0)
     i_lse = top + jnp.log(jnp.sum(sums * jnp.exp2(peaks - top[None]), axis=0)) * LOG2E
-
-    wait_bytes(st_recv.at[pl.ds(0, n_ctx - 1)], recv_sem.at[2])
-    st_recv[n_ctx - 1] = st_send[ctx]
-    got = st_recv[...]
-    peaks, sums = got[:, 0:4, :], got[:, 4:8, :]
-    top = jnp.max(peaks, axis=0)
-    lse = top + jnp.log(jnp.sum(sums * jnp.exp2(peaks - top[None]), axis=0)) * LOG2E
-    lse_send[...] = jnp.zeros_like(lse_send)
-    lse_send[0:4, :] = lse
-
-    @pl.loop(1, n_ctx)
-    def _(r):
-        pltpu.make_async_remote_copy(
-            lse_send, lse_recv.at[ctx], send_sem.at[3], recv_sem.at[3],
-            device_id=(ctx_peer(r), pb), device_id_type=MESH,
-        ).start()
-
-    tacc[...] = jnp.zeros_like(tacc)
-    wait_bytes(lse_recv.at[pl.ds(0, n_ctx - 1)], recv_sem.at[3])
-    lse_recv[ctx] = lse_send[...]
-    for i in range(n_ctx):
-        fac_ref[4 * i:4 * i + 4, :] = jnp.exp2(st_send[i, 0:4, :] - lse_recv[i, 0:4, :])
-    fact = fac_ref[...].T * (1.0 / lanes)
-    hi = fact.astype(BF16)
-    fact_hi[...] = hi.astype(F32)
-    fact_lo[...] = fact - hi.astype(F32)
-
-    @pl.loop(0, blocks)
-    def _(block):
-        lane = lax.broadcasted_iota(jnp.int32, (lanes, lanes), 1)
-        for i in range(QBLOCK):
-            here = lane == block * QBLOCK + i
-            f_ref[i * lanes:(i + 1) * lanes, 0:lanes] = jnp.where(here, fact_hi[...], 0.0).astype(BF16)
-            f_ref[i * lanes:(i + 1) * lanes, lanes:] = jnp.where(here, fact_lo[...], 0.0).astype(BF16)
-        tacc[...] += nn_dot(p_ref[block], f_ref[...])
 
     target = tacc[:, 0:lanes] + tacc[:, lanes:]
     log_index = logit_ref[...] - i_lse
@@ -271,6 +327,27 @@
             device_id=(ctx, peer), device_id_type=MESH,
         ).start()
 
+    wait_bytes(t_recv.at[pl.ds(0, n_ctx - 1)], recv_sem.at[5])
+    w_total = jnp.sum(t_recv[0:n_ctx - 1], axis=0) + t_send[ctx]
+    w_send[...] = w_total
+    kl_ref[...] = w_total[2:3, :]
+
+    @pl.loop(1, n_ctx)
+    def _(r):
+        pltpu.make_async_remote_copy(
+            w_send, w_recv.at[ctx], send_sem.at[9], recv_sem.at[9],
+            device_id=(ctx_peer(r), pb), device_id_type=MESH,
+        ).start()
+
+    wait_bytes(kp_recv, recv_sem.at[6])
+    own_quarter = kp_ref[pl.ds(pb * q_rows, q_rows), :] + kp_recv[0] + kp_recv[1] + kp_recv[2]
+    ko_ref[pb] = own_quarter
+    for r in range(1, n_pb):
+        pltpu.make_async_remote_copy(
+            ko_ref.at[pb], ko_ref.at[pb], send_sem.at[8], recv_sem.at[8],
+            device_id=(ctx, pb_peer(r)), device_id_type=MESH,
+        ).start()
+
     for r in range(1, ZGROUP):
         wait_bytes(dl_gather.at[r - 1], zd_sem.at[r - 1])
         dl_ref[r] = dl_gather[r - 1]
@@ -300,27 +377,6 @@
             device_id=(k * ZGROUP + z, pb), device_id_type=MESH,
         ).start()
 
-    wait_bytes(kp_recv, recv_sem.at[6])
-    own_quarter = kp_ref[pl.ds(pb * q_rows, q_rows), :] + kp_recv[0] + kp_recv[1] + kp_recv[2]
-    ko_ref[pb] = own_quarter
-    for r in range(1, n_pb):
-        pltpu.make_async_remote_copy(
-            ko_ref.at[pb], ko_ref.at[pb], send_sem.at[8], recv_sem.at[8],
-            device_id=(ctx, pb_peer(r)), device_id_type=MESH,
-        ).start()
-
-    wait_bytes(t_recv.at[pl.ds(0, n_ctx - 1)], recv_sem.at[5])
-    w_total = jnp.sum(t_recv[0:n_ctx - 1], axis=0) + t_send[ctx]
-    w_send[...] = w_total
-    kl_ref[...] = w_total[2:3, :]
-
-    @pl.loop(1, n_ctx)
-    def _(r):
-        pltpu.make_async_remote_copy(
-            w_send, w_recv.at[ctx], send_sem.at[9], recv_sem.at[9],
-            device_id=(ctx_peer(r), pb), device_id_type=MESH,
-        ).start()
-
     query_pair(n_grp - 1)
 
     wait_bytes(ko_ref.at[pl.ds(0, n_pb - 1)], recv_sem.at[8])
@@ -340,14 +396,20 @@
 
     wait_bytes(key_gather, send_sem.at[0])
     wait_bytes(ist_recv.at[pl.ds(0, n_ctx - 1)], send_sem.at[1])
-    wait_bytes(st_recv.at[pl.ds(0, n_ctx - 1)], send_sem.at[2])
-    wait_bytes(lse_recv.at[pl.ds(0, n_ctx - 1)], send_sem.at[3])
+    for part in range(2):
+        wait_bytes(st_recv.at[part, pl.ds(0, n_ctx - 1)], st_ssem.at[part])
+        wait_bytes(lse_recv.at[part, pl.ds(0, n_ctx - 1)], lse_ssem.at[part])
     wait_bytes(dl_gather, send_sem.at[4])
     wait_bytes(t_recv.at[pl.ds(0, n_ctx - 1)], send_sem.at[5])
     wait_bytes(kp_recv, send_sem.at[6])
     wait_bytes(q_recv, send_sem.at[7])
     wait_bytes(ko_ref.at[pl.ds(0, n_pb - 1)], send_sem.at[8])
     wait_bytes(w_recv.at[pl.ds(0, n_ctx - 1)], send_sem.at[9])
+
+
+def hand_on(*refs):
+    for source, target in zip(refs[:4], refs[4:]):
+        target[...] = source[...]
 
 
 def local(queries, key_cache, index_queries, index_keys, head_weights, positions, valid_lengths):
@@ -362,9 +424,11 @@
     vmem = pltpu.VMEM
     tile = (8, lanes)
     scratch = [
+        vmem((heads, q_rows, idim), BF16),
         vmem((2, QBLOCK, depth, lanes), BF16),
         vmem((t_rows, depth), BF16),
-        vmem((2, t_rows, 2 * lanes), F32),
+        vmem((t_rows, QBLOCK * lanes), F32),
+        vmem((8, 2 * lanes), F32),
         vmem((blocks, t_rows, QBLOCK * lanes), BF16),
         vmem((t_rows, lanes), F32),
         vmem((ZGROUP, t_rows, lanes), F32),
@@ -382,10 +446,10 @@
         vmem((ZGROUP - 1, t_rows, lanes), F32),
         vmem(tile, F32),
         vmem((n_ctx, *tile), F32),
-        vmem((n_ctx, *tile), F32),
-        vmem((n_ctx, *tile), F32),
-        vmem(tile, F32),
-        vmem((n_ctx, *tile), F32),
+        vmem((2, n_ctx, *tile), F32),
+        vmem((2, n_ctx, *tile), F32),
+        vmem((2, *tile), F32),
+        vmem((2, n_ctx, *tile), F32),
         vmem((t_rows, idim), F32),
         vmem((n_pb - 1, t_rows // n_pb, idim), F32),
         vmem((n_pb, t_rows // n_pb, idim), F32),
@@ -395,14 +459,16 @@
         vmem((n_ctx, *tile), F32),
         vmem((n_grp, 2, idim, lanes), F32),
         vmem((n_grp - 1, 2, idim, lanes), F32),
+        pltpu.SemaphoreType.DMA,
         pltpu.SemaphoreType.DMA((2,)),
         pltpu.SemaphoreType.DMA((10,)),
         pltpu.SemaphoreType.DMA((10,)),
         pltpu.SemaphoreType.DMA((ZGROUP - 1,)),
         pltpu.SemaphoreType.DMA((ZGROUP - 1,)),
-    ]
+    ] + [pltpu.SemaphoreType.DMA((2,))] * 4
     on_chip = pl.BlockSpec(memory_space=pltpu.VMEM)
-    kl, key_grad, query_grad, weight_grad = pl.pallas_call(
+    in_hbm = pl.BlockSpec(memory_space=pl.ANY)
+    results = pl.pallas_call(
         functools.partial(kernel, n_ctx, n_pb, loss_scale),
         out_shape=(
             jax.ShapeDtypeStruct((1, q_rows), F32),
@@ -410,14 +476,14 @@
             jax.ShapeDtypeStruct((heads // n_ctx, q_rows, idim), F32),
             jax.ShapeDtypeStruct((heads, q_rows), F32),
         ),
-        in_specs=[pl.BlockSpec(memory_space=pl.ANY)] + [on_chip] * 6,
+        in_specs=[in_hbm, on_chip, in_hbm] + [on_chip] * 4,
         out_specs=(on_chip,) * 4,
         scratch_shapes=scratch,
         compiler_params=pltpu.CompilerParams(
             collective_id=0, has_side_effects=True, vmem_limit_bytes=60 * 1024 * 1024
         ),
     )(
-        queries.transpose(0, 2, 1),
+        queries.transpose(0, 2, 1).reshape(n_ctx, OWNED, lat, lanes),
         key_cache.T,
         index_queries,
         index_keys,
@@ -425,6 +491,12 @@
         positions.reshape(1, q_rows),
         valid_lengths.reshape(1, q_rows),
     )
+    kl, key_grad, query_grad, weight_grad = pl.pallas_call(
+        hand_on,
+        out_shape=tuple(jax.ShapeDtypeStruct(x.shape, x.dtype) for x in results),
+        in_specs=[on_chip] * 4,
+        out_specs=(on_chip,) * 4,
+    )(*results)
     return kl.reshape(q_rows), key_grad, query_grad, weight_grad.T
 
 

time: 94.9 us -> 76.8 us (0.81); the launches traced: 94.6 us -> 75.4 us
  Pallas kernels: 88.2 us -> 74.7 us
  local copies, waits for them, and re-layouts: 5.73 us -> 0 us
    pallas_call x1, Pallas kernels: 88.2 us -> 73 us  [local(): pl.pallas_call(functools.partial(kernel, n_ctx, n_pb, loss_scale), out_sh...]
    unnamed x4 -> x0, local copies, waits for them, and re-layouts: 5.73 us -> none
    pallas_call x0 -> x1, Pallas kernels: none -> 1.76 us  [local(): pl.pallas_call(hand_on, out_shape=tuple((jax.ShapeDtypeStruct(x.shape, x....]
where the time goes in v2:
time: 76.8 us; the launch traced here: 75.4 us
  Pallas kernels  74.7 us (97%)
    pallas_call x1, Pallas kernels, local(): pl.pallas_call(functools.partial(kernel, n_ctx, n_pb, loss_scale), out_sh...  73 us
    pallas_call x1, Pallas kernels, local(): pl.pallas_call(hand_on, out_shape=tuple((jax.ShapeDtypeStruct(x.shape, x....  1.76 us

profile of v2, /device:TPU:0, one launch (start us, length us, event | category | flops | bytes accessed | tf_op | source)
XLA Modules:
  0.0 75.4 jit_solution(16195359737669342116)
XLA Ops:
  0.6 73.0 %shard_map.102 = (f32[1,128]{1,0:T(1,128)}, f32[512,128]{1,0:T(8,128)}, f32[2,128,128]{2,1,0:T(8,128)}, f32[64,128]{1,0:T(8,128)}) custom-call(bf16[32,4,576,128]{3,2,1,0:T(8,128)(2,1)} %bitcast.9, bf16[576,512]{1,0:T(8,128)(2,1)} %bitcast.10, bf16[64,128,128]{2,1,0:T(8,128)(2,1)} %iq_hbm.1, bf16[512,128]{1,0:T(8,128)(2,1)} %ik_ref.1, f32[64,128]{1,0:T(8,128)} %bitcast.11, ...), custom_call_target="tpu_custom_call" | custom-call | tf_op jit(solution)/shard_map/pallas_call | solution.py:471
  73.6 1.8 %shard_map.103 = (f32[1,128]{1,0:T(1,128)}, f32[512,128]{1,0:T(8,128)}, f32[2,128,128]{2,1,0:T(8,128)}, f32[64,128]{1,0:T(8,128)}) custom-call(f32[1,128]{1,0:T(1,128)} %get-tuple-element.12.refs_0_, f32[512,128]{1,0:T(8,128)} %get-tuple-element.13.refs_1_, f32[2,128,128]{2,1,0:T(8,128)} %get-tuple-element.14.refs_2_, f32[64,128]{1,0:T(8,128)} %get-tuple-element.15.refs_3_), custom_call_target="tpu_custom_call" | custom-call | tf_op jit(solution)/shard_map/pallas_call | solution.py:494

commit v3 on v2

v3 whole, which is shorter than its diff:
```python
import functools
import math

import jax
import jax.numpy as jnp
from jax import lax
from jax.experimental import pallas as pl
from jax.experimental.pallas import tpu as pltpu
from jax.sharding import PartitionSpec as P

NEG = -1e30
LOG2E = math.log2(math.e)
MESH = pl.DeviceIdType.MESH
F32 = jnp.float32
BF16 = jnp.bfloat16
ZGROUP = 4
QBLOCK = 8
KSPLIT = 5
TSTEP = 4
OWNED = 2


def nt_dot(lhs, rhs):
    return lax.dot_general(lhs, rhs, (((1,), (1,)), ((), ())), preferred_element_type=F32)


def nn_dot(lhs, rhs):
    return jnp.dot(lhs, rhs, preferred_element_type=F32)


def wait_bytes(ref, sem):
    pltpu.make_async_copy(ref, ref, sem).wait()


def kernel(
    n_ctx, n_pb, loss_scale,
    q_hbm, kt_hbm, iq_hbm, ik_ref, wt_ref, pos_ref, len_ref,
    kl_ref, key_ref, qg_ref, wg_ref,
    iq_ref, kt_ref, qb, ke, s_ref, peak_ref, p_ref, logit_ref, dl_ref, fac_ref, fact_hi, fact_lo, f_ref, tacc,
    ikt_all, ik_all, coef, coef2, w2_ref, relu_ref,
    key_send, key_gather, dl_send, dl_gather, dl_twice,
    ist_send, ist_recv, st_send, st_recv, lse_send, lse_recv,
    kp_ref, kc_ref, kh_ref, ko_ref, t_send, t_recv, w_send, w_recv, qs_ref, q_recv,
    iq_sem, kt_sem, q_sem, send_sem, recv_sem, zk_sem, zd_sem,
    st_ssem, st_rsem, lse_ssem, lse_rsem, zd_ssem, qr_ssem, qr_rsem, kp_ssem, kp_rsem,
):
    ctx = lax.axis_index("ctx")
    pb = lax.axis_index("pb")
    z = lax.rem(ctx, ZGROUP)
    grp = ctx // ZGROUP
    n_grp = n_ctx // ZGROUP
    heads = iq_ref.shape[0]
    pairs = heads // 2
    queries, lat, lanes = q_hbm.shape
    half_lanes = lanes // 2
    half_rows = ik_ref.shape[0] // 2
    t_rows = ik_ref.shape[0]
    idim = ik_ref.shape[1]
    blocks = queries // QBLOCK
    split = blocks // 2
    iscale = idim ** -0.5
    mscale = 192 ** -0.5 * LOG2E

    def ctx_peer(r):
        return lax.rem(ctx + r, n_ctx)

    def pb_peer(r):
        return lax.rem(pb + r, n_pb)

    def z_peer(r):
        return grp * ZGROUP + lax.rem(z + r, ZGROUP)

    def q_copy(block, slot):
        return pltpu.make_async_copy(
            q_hbm.at[pl.ds(block * QBLOCK, QBLOCK)],
            qb.at[slot, :, pl.ds(0, lat), :],
            q_sem.at[slot],
        )

    kt_copy = pltpu.make_async_copy(kt_hbm, kt_ref, kt_sem)
    kt_copy.start()
    q_copy(0, 0).start()
    q_copy(1, 1).start()
    iq_copy = pltpu.make_async_copy(iq_hbm, iq_ref, iq_sem)
    iq_copy.start()

    barrier = pltpu.get_barrier_semaphore()

    @pl.loop(1, n_ctx)
    def _(r):
        pl.semaphore_signal(barrier, inc=1, device_id=(ctx_peer(r), pb), device_id_type=MESH)

    @pl.loop(1, n_pb)
    def _(r):
        pl.semaphore_signal(barrier, inc=1, device_id=(ctx, pb_peer(r)), device_id_type=MESH)

    t_index = ctx * t_rows + lax.broadcasted_iota(jnp.int32, (t_rows, lanes), 0)
    pos = pos_ref[...]
    visible = (t_index <= pos) & (t_index > pos - len_ref[...])
    bias = jnp.where(visible, 0.0, NEG)
    hidden = ke.shape[1] - lanes
    kt_copy.wait()
    ke[:, 0:lat] = kt_ref[...].astype(F32).T.astype(BF16)
    ke[:, lat:hidden] = jnp.zeros((t_rows, hidden - lat), BF16)
    ke[:, hidden:] = bias.astype(BF16)
    for slot in range(2):
        for i in range(QBLOCK):
            qb[slot, i, lat:hidden, :] = jnp.zeros((hidden - lat, lanes), BF16)

    w_even = wt_ref[pl.ds(0, pairs, stride=2), :] * iscale
    w_odd = wt_ref[pl.ds(1, pairs, stride=2), :] * iscale
    first_lanes = lax.broadcasted_iota(jnp.int32, (pairs, lanes), 1) < half_lanes
    w2_ref[0] = jnp.where(first_lanes, w_even, pltpu.roll(w_odd, half_lanes, 1))
    w2_ref[1] = jnp.where(first_lanes, pltpu.roll(w_even, half_lanes, 1), w_odd)

    ik = ik_ref[...]
    key_send[...] = ik.astype(F32)

    pl.semaphore_wait(barrier, n_ctx - 1 + n_pb - 1)

    for r in range(1, ZGROUP):
        pltpu.make_async_remote_copy(
            key_send, key_gather.at[r - 1], send_sem.at[0], zk_sem.at[r - 1],
            device_id=(z_peer(r), pb), device_id_type=MESH,
        ).start()

    st_send[...] = jnp.zeros_like(st_send)

    def exponentials(block):
        part = block // split
        for u in range(QBLOCK // 2):
            peak = peak_ref[u:u + 1, :]
            expo = jnp.exp2(s_ref[:, 2 * u * lanes:(2 * u + 2) * lanes] * mscale - peak)
            total = jnp.sum(expo, axis=0, keepdims=True)
            p_ref[block, :, 2 * u * lanes:(2 * u + 2) * lanes] = expo.astype(BF16)
            for h in range(2):
                i = 2 * u + h
                owner = QBLOCK // OWNED * lax.rem(block, split) + i // OWNED
                st_send[part, owner, pl.ds(i % OWNED, 1), :] = peak[:, h * lanes:(h + 1) * lanes]
                st_send[part, owner, pl.ds(4 + i % OWNED, 1), :] = total[:, h * lanes:(h + 1) * lanes]

    def scores(block):
        slot = lax.rem(block, 2)
        q_copy(block, slot).wait()
        row = lax.broadcasted_iota(jnp.int32, (lanes, lanes), 0)
        for i in range(QBLOCK):
            qb[slot, i, hidden:, :] = jnp.where(row == block * QBLOCK + i, 1.0, 0.0).astype(BF16)
        exponentials(lax.max(block - 1, 0))
        rhs = jnp.concatenate([qb[slot, i] for i in range(QBLOCK)], axis=1)
        s = nn_dot(ke[...], rhs)
        s_ref[...] = s
        peak = jnp.max(s, axis=0, keepdims=True) * mscale
        for u in range(QBLOCK // 2):
            peak_ref[u:u + 1, :] = peak[:, 2 * u * lanes:(2 * u + 2) * lanes]

        @pl.when(block + 2 < blocks)
        def _():
            q_copy(block + 2, slot).start()

    def send_stats(part):
        @pl.loop(1, n_ctx)
        def _(r):
            peer = ctx_peer(r)
            pltpu.make_async_remote_copy(
                st_send.at[part, peer], st_recv.at[part, r - 1], st_ssem.at[part], st_rsem.at[part],
                device_id=(peer, pb), device_id_type=MESH,
            ).start()

    def combine(part):
        wait_bytes(st_recv.at[part, pl.ds(0, n_ctx - 1)], st_rsem.at[part])
        st_recv[part, n_ctx - 1] = st_send[part, ctx]
        got = st_recv[part]
        peaks, sums = got[:, 0:4, :], got[:, 4:8, :]
        top = jnp.max(peaks, axis=0)
        total = jnp.sum(sums * jnp.exp2(peaks - top[None]), axis=0)
        lse_send[part] = jnp.zeros((8, lanes), F32)
        lse_send[part, 0:4, :] = top + jnp.log(jnp.maximum(total, 1e-30)) * LOG2E

        @pl.loop(1, n_ctx)
        def _(r):
            pltpu.make_async_remote_copy(
                lse_send.at[part], lse_recv.at[part, ctx], lse_ssem.at[part], lse_rsem.at[part],
                device_id=(ctx_peer(r), pb), device_id_type=MESH,
            ).start()

    def factors(part):
        wait_bytes(lse_recv.at[part, pl.ds(0, n_ctx - 1)], lse_rsem.at[part])
        lse_recv[part, ctx] = lse_send[part]
        for i in range(n_ctx):
            row = part * OWNED * n_ctx + OWNED * i
            fac_ref[row:row + OWNED, :] = jnp.exp2(
                st_send[part, i, 0:OWNED, :] - lse_recv[part, i, 0:OWNED, :]
            )
        fact = fac_ref[...].T * (1.0 / lanes)
        hi = fact.astype(BF16)
        fact_hi[...] = hi.astype(F32)
        fact_lo[...] = fact - hi.astype(F32)

    @pl.loop(0, split + 1)
    def _(block):
        scores(block)

    send_stats(0)

    @pl.loop(split + 1, blocks)
    def _(block):
        scores(block)

    exponentials(blocks - 1)
    send_stats(1)
    combine(0)

    iq_copy.wait()
    logit_ref[...] = jnp.zeros_like(logit_ref)

    @pl.loop(0, pairs // 4)
    def _(step):
        total = logit_ref[...]
        for u in range(4):
            jp = step * 4 + u
            raw = nt_dot(ik, iq_ref[pl.ds(2 * jp, 2)].reshape(2 * lanes, idim))
            w = wt_ref[pl.ds(2 * jp, 2), :]
            active = jnp.maximum(raw, 0.0)
            relu_ref[jp] = active
            total = total + active[:, :lanes] * w[0:1]
            total = total + active[:, lanes:] * w[1:2]
        logit_ref[...] = total

    logits = logit_ref[...] * (iscale * LOG2E) + bias
    logit_ref[...] = logits
    i_peak = jnp.max(logits, axis=0, keepdims=True)
    i_sum = jnp.sum(jnp.exp2(logits - i_peak), axis=0, keepdims=True)
    ist_send[...] = jnp.zeros_like(ist_send)
    ist_send[0:1, :] = i_peak
    ist_send[1:2, :] = i_sum

    @pl.loop(1, n_ctx)
    def _(r):
        pltpu.make_async_remote_copy(
            ist_send, ist_recv.at[r - 1], send_sem.at[1], recv_sem.at[1],
            device_id=(ctx_peer(r), pb), device_id_type=MESH,
        ).start()

    combine(1)

    ik_all[0:t_rows, :] = ik
    ikt_all[:, 0:t_rows] = key_send[...].T.astype(BF16)
    for r in range(1, ZGROUP):
        wait_bytes(key_gather.at[r - 1], zk_sem.at[r - 1])
        got = key_gather[r - 1]
        ik_all[r * t_rows:(r + 1) * t_rows, :] = got.astype(BF16)
        ikt_all[:, r * t_rows:(r + 1) * t_rows] = got.T.astype(BF16)

    tacc[...] = jnp.zeros_like(tacc)

    def add_target(step):
        lane = lax.broadcasted_iota(jnp.int32, (lanes, lanes), 1)
        for i in range(TSTEP * QBLOCK):
            here = lane == step * (TSTEP * QBLOCK) + i
            f_ref[i * lanes:(i + 1) * lanes, 0:lanes] = jnp.where(here, fact_hi[...], 0.0).astype(BF16)
            f_ref[i * lanes:(i + 1) * lanes, lanes:] = jnp.where(here, fact_lo[...], 0.0).astype(BF16)
        wide = jnp.concatenate([p_ref[TSTEP * step + u] for u in range(TSTEP)], axis=1)
        tacc[...] += nn_dot(wide, f_ref[...])

    lower = lax.broadcasted_iota(jnp.int32, (half_rows, lanes), 1) < half_lanes

    def swap(x):
        return pltpu.roll(x, half_lanes, 1)

    def send_dlogit(half, dl):
        top, bottom = dl[:half_rows], dl[half_rows:]
        if half == 0:
            dl_send[half] = jnp.where(lower, top, swap(bottom))
        else:
            dl_send[half] = jnp.where(lower, swap(top), bottom)
        for r in range(1, ZGROUP):
            pltpu.make_async_remote_copy(
                dl_send.at[half], dl_gather.at[half, r - 1], zd_ssem.at[half], zd_sem.at[half, r - 1],
                device_id=(z_peer(r), pb), device_id_type=MESH,
            ).start()

    factors(0)

    @pl.loop(0, split // TSTEP)
    def _(step):
        add_target(step)

    wait_bytes(ist_recv.at[pl.ds(0, n_ctx - 1)], recv_sem.at[1])
    ist_recv[n_ctx - 1] = ist_send[...]
    got = ist_recv[...]
    peaks, sums = got[:, 0:1, :], got[:, 1:2, :]
    top = jnp.max(peaks, axis=0)
    i_lse = top + jnp.log(jnp.sum(sums * jnp.exp2(peaks - top[None]), axis=0)) * LOG2E

    index_prob = jnp.exp2(logit_ref[...] - i_lse)
    send_dlogit(0, loss_scale * (index_prob - (tacc[:, 0:lanes] + tacc[:, lanes:])))

    factors(1)

    @pl.loop(split // TSTEP, blocks // TSTEP)
    def _(step):
        add_target(step)

    target = tacc[:, 0:lanes] + tacc[:, lanes:]
    log_index = logit_ref[...] - i_lse
    index_prob = jnp.exp2(log_index)
    dl_ref[...] = loss_scale * (index_prob - target)
    send_dlogit(1, dl_ref[...])
    positive = target > 0
    log_target = jnp.log(jnp.where(positive, target, 1.0))
    kl = jnp.sum(
        jnp.where(positive, target * (log_target - log_index * math.log(2.0)), 0.0), axis=0, keepdims=True
    )

    kp_ref[...] = jnp.zeros_like(kp_ref)

    def key_step(step):
        dl = dl_ref[...]
        for u in range(4):
            jp = step * 4 + u
            w = wt_ref[pl.ds(2 * jp, 2), :] * iscale
            for h in range(2):
                part = relu_ref[jp, :, h * lanes:(h + 1) * lanes]
                t_send[jp, pl.ds(h, 1), :] = jnp.sum(dl * part, axis=0, keepdims=True) * iscale
                coef[:, (2 * u + h) * lanes:(2 * u + h + 1) * lanes] = jnp.where(
                    part > 0, dl * w[h:h + 1], 0.0
                ).astype(BF16)
            t_send[jp, pl.ds(2, 1), :] = kl
            t_send[jp, pl.ds(3, 5), :] = jnp.zeros((5, lanes), F32)
        kp_ref[...] += nn_dot(coef[...], iq_ref[pl.ds(8 * step, 8)].reshape(8 * lanes, idim))

    @pl.loop(0, KSPLIT)
    def _(step):
        key_step(step)

    def query_half(half, between):
        for r in range(ZGROUP):
            if r:
                wait_bytes(dl_gather.at[half, r - 1], zd_sem.at[half, r - 1])
            packed = dl_gather[half, r - 1] if r else dl_send[half]
            other = swap(packed)
            dl_twice[r, 0:half_rows, :] = jnp.where(lower, packed, other)
            dl_twice[r, half_rows:, :] = jnp.where(lower, other, packed)

        def share(k):
            return k * ZGROUP + z

        def iq_half(k):
            part = iq_ref[pl.ds(2 * share(k), 2), half * half_lanes:(half + 1) * half_lanes, :]
            return part.reshape(lanes, idim)

        def two_peers(step, u):
            ks = [lax.rem(grp + 1 + 2 * step + i, n_grp) for i in range(2)]
            rhs = jnp.concatenate([iq_half(k) for k in ks], axis=0)
            ws = [w2_ref[half, pl.ds(share(k), 1), :] for k in ks]
            for r in range(ZGROUP):
                raw = nt_dot(ik_all[r * t_rows:(r + 1) * t_rows, :], rhs)
                dl = dl_twice[r]
                for i in range(2):
                    coef2[u, r * t_rows:(r + 1) * t_rows, i * lanes:(i + 1) * lanes] = jnp.where(
                        raw[:, i * lanes:(i + 1) * lanes] > 0, dl * ws[i], 0.0
                    ).astype(BF16)
            grad = nn_dot(ikt_all[...], coef2[u])
            for i in range(2):
                qs_ref[half, 2 * step + i] = grad[:, i * lanes:(i + 1) * lanes]

        def send(slot):
            k = lax.rem(grp + 1 + slot, n_grp)
            pltpu.make_async_remote_copy(
                qs_ref.at[half, slot], q_recv.at[half, slot], qr_ssem.at[half], qr_rsem.at[half],
                device_id=(share(k), pb), device_id_type=MESH,
            ).start()

        @pl.loop(0, n_grp // 4)
        def _(step):
            two_peers(2 * step, 0)
            send(4 * step)
            send(4 * step + 1)
            two_peers(2 * step + 1, 1)
            send(4 * step + 2)

            @pl.when(step < n_grp // 4 - 1)
            def _():
                send(4 * step + 3)
                if between is not None:
                    between()

    query_half(0, None)

    @pl.loop(KSPLIT, pairs // 4)
    def _(step):
        key_step(step)

    @pl.loop(1, n_ctx)
    def _(r):
        peer = ctx_peer(r)
        pltpu.make_async_remote_copy(
            t_send.at[peer], t_recv.at[r - 1], send_sem.at[5], recv_sem.at[5],
            device_id=(peer, pb), device_id_type=MESH,
        ).start()

    core = lax.rem(pb, 2)
    mate = pb + 1 - 2 * core
    across = lax.rem(pb + 2, n_pb)
    own_rows = pl.ds(core * half_rows, half_rows)
    pltpu.make_async_remote_copy(
        kp_ref.at[pl.ds((1 - core) * half_rows, half_rows)], kc_ref, kp_ssem.at[0], kp_rsem.at[0],
        device_id=(ctx, mate), device_id_type=MESH,
    ).start()


    def hand_round():
        wait_bytes(t_recv.at[pl.ds(0, n_ctx - 1)], recv_sem.at[5])
        w_total = jnp.sum(t_recv[0:n_ctx - 1], axis=0) + t_send[ctx]
        w_send[...] = w_total
        kl_ref[...] = w_total[2:3, :]

        @pl.loop(1, n_ctx)
        def _(r):
            pltpu.make_async_remote_copy(
                w_send, w_recv.at[ctx], send_sem.at[9], recv_sem.at[9],
                device_id=(ctx_peer(r), pb), device_id_type=MESH,
            ).start()

    def key_across():
        wait_bytes(kc_ref, kp_rsem.at[0])
        kh_ref[0] = kp_ref[own_rows, :] + kc_ref[...]
        pltpu.make_async_remote_copy(
            kh_ref.at[0], kh_ref.at[1], kp_ssem.at[1], kp_rsem.at[1],
            device_id=(ctx, across), device_id_type=MESH,
        ).start()
        hand_round()

    query_half(1, key_across)

    wait_bytes(kh_ref.at[1], kp_rsem.at[1])
    ko_ref[core] = kh_ref[0] + kh_ref[1]
    pltpu.make_async_remote_copy(
        ko_ref.at[core], ko_ref.at[core], kp_ssem.at[2], kp_rsem.at[2],
        device_id=(ctx, mate), device_id_type=MESH,
    ).start()

    wait_bytes(w_recv.at[pl.ds(0, n_ctx - 1)], recv_sem.at[9])
    w_recv[ctx] = w_send[...]
    for i in range(n_ctx):
        wg_ref[2 * i:2 * i + 2, :] = w_recv[i, 0:2, :]

    for half in range(2):
        wait_bytes(q_recv.at[half], qr_rsem.at[half])
        total = qs_ref[half, n_grp - 1]
        for k in range(n_grp - 1):
            total = total + q_recv[half, k]
        total = total.T
        for h in range(2):
            qg_ref[h, half * half_lanes:(half + 1) * half_lanes, :] = total[h * half_lanes:(h + 1) * half_lanes]

    wait_bytes(ko_ref.at[0], kp_rsem.at[2])
    for i in range(2):
        key_ref[i * half_rows:(i + 1) * half_rows, :] = ko_ref[i]

    wait_bytes(kc_ref, kp_ssem.at[0])
    wait_bytes(kc_ref, kp_ssem.at[1])
    wait_bytes(kc_ref, kp_ssem.at[2])
    wait_bytes(key_gather, send_sem.at[0])
    wait_bytes(ist_recv.at[pl.ds(0, n_ctx - 1)], send_sem.at[1])
    for part in range(2):
        wait_bytes(st_recv.at[part, pl.ds(0, n_ctx - 1)], st_ssem.at[part])
        wait_bytes(lse_recv.at[part, pl.ds(0, n_ctx - 1)], lse_ssem.at[part])
        wait_bytes(dl_gather.at[part], zd_ssem.at[part])
        wait_bytes(q_recv.at[part], qr_ssem.at[part])
    wait_bytes(t_recv.at[pl.ds(0, n_ctx - 1)], send_sem.at[5])
    wait_bytes(w_recv.at[pl.ds(0, n_ctx - 1)], send_sem.at[9])


def hand_on(*refs):
    for source, target in zip(refs[:4], refs[4:]):
        target[...] = source[...]


def local(queries, key_cache, index_queries, index_keys, head_weights, positions, valid_lengths):
    n_ctx, n_pb = lax.axis_size("ctx"), lax.axis_size("pb")
    q_rows, lanes, lat = queries.shape
    t_rows, idim = index_keys.shape
    heads = index_queries.shape[0]
    blocks = q_rows // QBLOCK
    n_grp = n_ctx // ZGROUP
    depth = -(-(lanes + lat) // 256) * 256
    loss_scale = t_rows * n_ctx / (q_rows * n_pb)
    vmem = pltpu.VMEM
    tile = (8, lanes)
    scratch = [
        vmem((heads, q_rows, idim), BF16),
        vmem((lat, t_rows), BF16),
        vmem((2, QBLOCK, depth, lanes), BF16),
        vmem((t_rows, depth), BF16),
        vmem((t_rows, QBLOCK * lanes), F32),
        vmem((8, 2 * lanes), F32),
        vmem((blocks, t_rows, QBLOCK * lanes), BF16),
        vmem((t_rows, lanes), F32),
        vmem((t_rows, lanes), F32),
        vmem((q_rows, lanes), F32),
        vmem((lanes, q_rows), F32),
        vmem((lanes, q_rows), F32),
        vmem((TSTEP * QBLOCK * lanes, 2 * lanes), BF16),
        vmem((t_rows, 2 * lanes), F32),
        vmem((idim, ZGROUP * t_rows), BF16),
        vmem((ZGROUP * t_rows, idim), BF16),
        vmem((t_rows, 8 * lanes), BF16),
        vmem((2, ZGROUP * t_rows, 2 * lanes), BF16),
        vmem((2, heads // 2, lanes), F32),
        vmem((heads // 2, t_rows, 2 * lanes), F32),
        vmem((t_rows, idim), F32),
        vmem((ZGROUP - 1, t_rows, idim), F32),
        vmem((2, t_rows // 2, lanes), F32),
        vmem((2, ZGROUP - 1, t_rows // 2, lanes), F32),
        vmem((ZGROUP, t_rows, lanes), F32),
        vmem(tile, F32),
        vmem((n_ctx, *tile), F32),
        vmem((2, n_ctx, *tile), F32),
        vmem((2, n_ctx, *tile), F32),
        vmem((2, *tile), F32),
        vmem((2, n_ctx, *tile), F32),
        vmem((t_rows, idim), F32),
        vmem((t_rows // 2, idim), F32),
        vmem((2, t_rows // 2, idim), F32),
        vmem((2, t_rows // 2, idim), F32),
        vmem((n_ctx, *tile), F32),
        vmem((n_ctx, *tile), F32),
        vmem(tile, F32),
        vmem((n_ctx, *tile), F32),
        vmem((2, n_grp, idim, lanes), F32),
        vmem((2, n_grp - 1, idim, lanes), F32),
        pltpu.SemaphoreType.DMA,
        pltpu.SemaphoreType.DMA,
        pltpu.SemaphoreType.DMA((2,)),
        pltpu.SemaphoreType.DMA((10,)),
        pltpu.SemaphoreType.DMA((10,)),
        pltpu.SemaphoreType.DMA((ZGROUP - 1,)),
        pltpu.SemaphoreType.DMA((2, ZGROUP - 1)),
    ] + [pltpu.SemaphoreType.DMA((2,))] * 7 + [pltpu.SemaphoreType.DMA((3,))] * 2
    on_chip = pl.BlockSpec(memory_space=pltpu.VMEM)
    in_hbm = pl.BlockSpec(memory_space=pl.ANY)
    results = pl.pallas_call(
        functools.partial(kernel, n_ctx, n_pb, loss_scale),
        out_shape=(
            jax.ShapeDtypeStruct((1, q_rows), F32),
            jax.ShapeDtypeStruct((t_rows, idim), F32),
            jax.ShapeDtypeStruct((heads // n_ctx, q_rows, idim), F32),
            jax.ShapeDtypeStruct((heads, q_rows), F32),
        ),
        in_specs=[in_hbm, in_hbm, in_hbm] + [on_chip] * 4,
        out_specs=(on_chip,) * 4,
        scratch_shapes=scratch,
        compiler_params=pltpu.CompilerParams(
            collective_id=0, has_side_effects=True, vmem_limit_bytes=60 * 1024 * 1024
        ),
    )(
        queries.transpose(0, 2, 1),
        key_cache.T,
        index_queries,
        index_keys,
        head_weights.T,
        positions.reshape(1, q_rows),
        valid_lengths.reshape(1, q_rows),
    )
    kl, key_grad, query_grad, weight_grad = pl.pallas_call(
        hand_on,
        out_shape=tuple(jax.ShapeDtypeStruct(x.shape, x.dtype) for x in results),
        in_specs=[on_chip] * 4,
        out_specs=(on_chip,) * 4,
    )(*results)
    return kl.reshape(q_rows), key_grad, query_grad, weight_grad.T


def solution(mesh):
    in_specs = (
        P("pb", None, None),
        P("ctx", None),
        P(None, "pb", None),
        P("ctx", None),
        P("pb", None),
        P("pb"),
        P("pb"),
    )
    out_specs = (P("pb"), P("ctx", None), P("ctx", "pb", None), P("pb", None))
    return jax.shard_map(local, mesh=mesh, in_specs=in_specs, out_specs=out_specs, check_vma=False)
```

time: 76.8 us -> 68.6 us (0.89); the launches traced: 75.4 us -> 68.2 us
  Pallas kernels: 74.7 us -> 67.6 us
    pallas_call x1, Pallas kernels: 73 us -> 65.8 us  [local(): pl.pallas_call(functools.partial(kernel, n_ctx, n_pb, loss_scale), out_sh...]
where the time goes in v3:
time: 68.6 us; the launch traced here: 68.2 us
  Pallas kernels  67.6 us (99%)
    pallas_call x1, Pallas kernels, local(): pl.pallas_call(functools.partial(kernel, n_ctx, n_pb, loss_scale), out_sh...  65.8 us
    pallas_call x1, Pallas kernels, local(): pl.pallas_call(hand_on, out_shape=tuple((jax.ShapeDtypeStruct(x.shape, x....  1.76 us

profile of v3, /device:TPU:0, one launch (start us, length us, event | category | flops | bytes accessed | tf_op | source)
XLA Modules:
  0.0 68.2 jit_solution(1267341784790762766)
XLA Ops:
  0.6 65.8 %shard_map.102 = (f32[1,128]{1,0:T(1,128)}, f32[512,128]{1,0:T(8,128)}, f32[2,128,128]{2,1,0:T(8,128)}, f32[64,128]{1,0:T(8,128)}) custom-call(bf16[128,576,128]{2,1,0:T(8,128)(2,1)} %bitcast.7, bf16[576,512]{1,0:T(8,128)(2,1)} %bitcast.8, bf16[64,128,128]{2,1,0:T(8,128)(2,1)} %iq_hbm.1, bf16[512,128]{1,0:T(8,128)(2,1)} %ik_ref.1, f32[64,128]{1,0:T(8,128)} %bitcast.9, ...), custom_call_target="tpu_custom_call" | custom-call | tf_op jit(solution)/shard_map/pallas_call | solution.py:543
  66.4 1.8 %shard_map.103 = (f32[1,128]{1,0:T(1,128)}, f32[512,128]{1,0:T(8,128)}, f32[2,128,128]{2,1,0:T(8,128)}, f32[64,128]{1,0:T(8,128)}) custom-call(f32[1,128]{1,0:T(1,128)} %get-tuple-element.12.refs_0_, f32[512,128]{1,0:T(8,128)} %get-tuple-element.13.refs_1_, f32[2,128,128]{2,1,0:T(8,128)} %get-tuple-element.14.refs_2_, f32[64,128]{1,0:T(8,128)} %get-tuple-element.15.refs_3_), custom_call_target="tpu_custom_call" | custom-call | tf_op jit(solution)/shard_map/pallas_call | solution.py:566

commit v4 on v3

--- a/solution.py
+++ b/solution.py
@@ -16,7 +16,7 @@
 ZGROUP = 4
 QBLOCK = 8
 KSPLIT = 5
-TSTEP = 4
+TSTEP = 8
 OWNED = 2
 
 

time: 68.6 us -> 69.8 us (1.017)
  Pallas kernels: 67.6 us -> 68.4 us
    pallas_call x1, Pallas kernels: 65.8 us -> 66.6 us  [local(): pl.pallas_call(functools.partial(kernel, n_ctx, n_pb, loss_scale), out_sh...]
where the time goes in v4:
time: 69.8 us; the launch traced here: 69 us
  Pallas kernels  68.4 us (98%)
    pallas_call x1, Pallas kernels, local(): pl.pallas_call(functools.partial(kernel, n_ctx, n_pb, loss_scale), out_sh...  66.6 us
    pallas_call x1, Pallas kernels, local(): pl.pallas_call(hand_on, out_shape=tuple((jax.ShapeDtypeStruct(x.shape, x....  1.76 us

profile of v4, /device:TPU:0, one launch (start us, length us, event | category | flops | bytes accessed | tf_op | source)
XLA Modules:
  0.0 69.0 jit_solution(13485508793953278170)
XLA Ops:
  0.6 66.6 %shard_map.102 = (f32[1,128]{1,0:T(1,128)}, f32[512,128]{1,0:T(8,128)}, f32[2,128,128]{2,1,0:T(8,128)}, f32[64,128]{1,0:T(8,128)}) custom-call(bf16[128,576,128]{2,1,0:T(8,128)(2,1)} %bitcast.7, bf16[576,512]{1,0:T(8,128)(2,1)} %bitcast.8, bf16[64,128,128]{2,1,0:T(8,128)(2,1)} %iq_hbm.1, bf16[512,128]{1,0:T(8,128)(2,1)} %ik_ref.1, f32[64,128]{1,0:T(8,128)} %bitcast.9, ...), custom_call_target="tpu_custom_call" | custom-call | tf_op jit(solution)/shard_map/pallas_call | solution.py:543
  67.3 1.8 %shard_map.103 = (f32[1,128]{1,0:T(1,128)}, f32[512,128]{1,0:T(8,128)}, f32[2,128,128]{2,1,0:T(8,128)}, f32[64,128]{1,0:T(8,128)}) custom-call(f32[1,128]{1,0:T(1,128)} %get-tuple-element.12.refs_0_, f32[512,128]{1,0:T(8,128)} %get-tuple-element.13.refs_1_, f32[2,128,128]{2,1,0:T(8,128)} %get-tuple-element.14.refs_2_, f32[64,128]{1,0:T(8,128)} %get-tuple-element.15.refs_3_), custom_call_target="tpu_custom_call" | custom-call | tf_op jit(solution)/shard_map/pallas_call | solution.py:566
